TPU v7x, 32 devices: a whole 2x2x4 slice. The times are simulated.
32 devices in a mesh: band: 2 (over x), tile: 16 (over z, y, core).
Axes of the slice: x: 2, y: 2, z: 4, core: 2. Of those that a mesh axis runs over, the one named last changes fastest.
Arguments:
- visibilities: bfloat16 [1024, 8, 128], P(('band', 'tile')), parts along dimension 0, may hold values from -6 to 6
- screens: bfloat16 [394, 2, 8, 1024], P('band'), parts along dimension 0, may hold values from -0.9 to 1.5
- positions: float32 [197, 3], replicated, may hold values from -90 to 90
- channel_freq: float32 [128], P('band'), parts along dimension 0, may hold values from 0.9 to 1.1
- owner_tile: int32 [1024, 1], P(('band', 'tile')), parts along dimension 0, may hold values from 0 to 15; in each aligned block of 32 rows (0 to 31, 32 to 63, ...) at most 4 rows name the same one
- baseline: int32 [1024], P(('band', 'tile')), parts along dimension 0, may hold values from 0 to 19305
- time_block: int32 [1024], P(('band', 'tile')), parts along dimension 0, may hold values from 0 to 15
- row_in_tile: int32 [1024], P(('band', 'tile')), parts along dimension 0, may hold values from 0 to 31
- col_offset: int32 [1024], P(('band', 'tile')), parts along dimension 0, may hold values from 0 to 992
- valid_steps: int32 [1024], P(('band', 'tile')), parts along dimension 0, may hold values from 1 to 2
Outputs:
- grid: float32 [16, 512, 1024], P('band', 'tile'), parts along dimension 0
There are 2 independent parts, one for each index of `band`. A program takes and returns all parts, laid end to end along the dimension named above; an argument that names none is the same for every part. Nothing has to cross between parts.
Inputs may be any that keep to these rules, and one draw needn't show every extreme that they name: `owner_tile`: in each aligned block of 32 items (the items of one device) no tile is named by more than 4 items.
All inputs are finite; a program needn't handle non-finite values.
Results may differ from a plain program's by a relative error of at most 0.0037.
Values may be sent and summed in bfloat16 or wider, within the bound.
No kernel may reach another device: no remote copies, remote signals or barrier semaphores. Data moves between devices by JAX's collectives and lax.ppermute only.
A program may use at most 128 MiB of HBM per device.

v0:
```python
import math

import jax
import jax.numpy as jnp
from jax import lax
from jax.sharding import PartitionSpec as P

SUB = 32
CH = 64
NT = 2
BPER = 8
STRIP = 32
GCOLS = 1024


hour_step = 0.003
declination = -0.5
full_circle = 2.0 * math.pi


def padded(cells, sides, width):
    for axis, dim in sides:
        count = lax.axis_size(axis)
        ends = count - 1
        head = lax.slice_in_dim(cells, 0, width, axis=dim)
        tail = lax.slice_in_dim(cells, cells.shape[dim] - width, cells.shape[dim], axis=dim)
        cells = jnp.concatenate(
            [
                lax.ppermute(tail, axis, [(i, (i + 1) % count) for i in range(ends)]),
                cells,
                lax.ppermute(head, axis, [((i + 1) % count, i) for i in range(ends)]),
            ],
            axis=dim,
        )
    return cells


def station_pair(baseline_ids, stations):
    series = jnp.arange(stations, dtype=jnp.int32)
    offsets = series * (2 * stations - series - 1) // 2
    station_one = jnp.sum((offsets[None, :] <= baseline_ids[:, None]).astype(jnp.int32), axis=1) - 1
    station_two = (
        baseline_ids - station_one * (2 * stations - station_one - 1) // 2 + station_one + 1
    )
    return (station_one, station_two.astype(jnp.int32))


def uv_track(baseline_vec, angles):
    east_part = baseline_vec[:, 0:1]
    north_part = baseline_vec[:, 1:2]
    upward = baseline_vec[:, 2:3]
    sine_part = jnp.sin(angles)
    cosine = jnp.cos(angles)
    u_track = sine_part * east_part + cosine * north_part
    v_track = (
        -math.sin(declination) * cosine * east_part
        + math.sin(declination) * sine_part * north_part
        + math.cos(declination) * upward
    )
    return (u_track, v_track)


def phase_tables(visibilities, item_records, positions, channel_freq, stations):
    number = visibilities.shape[0]
    vis_width = NT * CH
    station_one, station_two = station_pair(item_records[:, 0], stations)
    baseline_vec = positions[station_two] - positions[station_one]
    tick_index = item_records[:, 1]
    start_time = (tick_index * NT).astype(positions.dtype)
    step_index = jnp.arange(NT).astype(positions.dtype)
    angles = hour_step * (start_time[:, None] + step_index[None, :])
    middle = hour_step * (start_time[:, None] + 0.5 * (NT - 1))
    u_now, v_now = uv_track(baseline_vec, angles)
    u_mid, v_mid = uv_track(baseline_vec, middle)
    u_delta = (u_now[:, :, None] * channel_freq[None, None, :] - u_mid[:, :, None]).reshape(
        number, vis_width
    )
    v_delta = (v_now[:, :, None] * channel_freq[None, None, :] - v_mid[:, :, None]).reshape(
        number, vis_width
    )
    live_mask = (jnp.arange(NT, dtype=jnp.int32)[None, :] < item_records[:, 4:5]).astype(
        positions.dtype
    )
    live_mask = jnp.broadcast_to(live_mask[:, :, None], (number, NT, CH)).reshape(number, vis_width)
    pixel_pos = (jnp.arange(SUB).astype(positions.dtype) - SUB // 2) / SUB
    angle_x = full_circle * pixel_pos[None, :, None] * u_delta[:, None, :]
    east_phase_table = jnp.concatenate([jnp.cos(angle_x), jnp.sin(angle_x)], axis=1).astype(
        jnp.bfloat16
    )
    angle_y = full_circle * pixel_pos[None, :, None] * v_delta[:, None, :]
    phase_real = jnp.cos(angle_y)
    phase_imag = jnp.sin(angle_y)
    samples = (
        visibilities.astype(positions.dtype).reshape(number, 4, 2, vis_width)
        * live_mask[:, None, None, :]
    )
    vis_real = samples[:, :, 0]
    vis_imag = samples[:, :, 1]
    weight_real = (
        phase_real[:, None] * vis_real[:, :, None] - phase_imag[:, None] * vis_imag[:, :, None]
    )
    weight_imag = (
        phase_real[:, None] * vis_imag[:, :, None] + phase_imag[:, None] * vis_real[:, :, None]
    )
    weighted_samples = (
        jnp.stack([weight_real, weight_imag], axis=2)
        .reshape(number, 8 * SUB, vis_width)
        .astype(jnp.bfloat16)
    )
    interval = (tick_index // BPER).astype(jnp.int32)
    return (east_phase_table, weighted_samples, station_one, station_two, interval)


def correct(jones_products, screens, station_one, station_two, interval):
    number = jones_products.shape[0]
    intervals = screens.shape[1]
    split_parts = jones_products.reshape(number, 2, SUB, 4, 2, SUB)
    sky_real = split_parts[:, 0, :, :, 0] - split_parts[:, 1, :, :, 1]
    sky_imag = split_parts[:, 0, :, :, 1] + split_parts[:, 1, :, :, 0]
    sky_real = jnp.transpose(sky_real, (0, 2, 1, 3)).reshape(number, 2, 2, SUB * SUB)
    sky_imag = jnp.transpose(sky_imag, (0, 2, 1, 3)).reshape(number, 2, 2, SUB * SUB)
    screen_table = screens.reshape(screens.shape[0] * intervals, 8, SUB * SUB)
    left_jones = (
        screen_table[station_one * intervals + interval]
        .astype(jones_products.dtype)
        .reshape(number, 2, 2, 2, SUB * SUB)
    )
    right_jones = (
        screen_table[station_two * intervals + interval]
        .astype(jones_products.dtype)
        .reshape(number, 2, 2, 2, SUB * SUB)
    )
    left_real = left_jones[:, :, :, 0]
    left_imag = left_jones[:, :, :, 1]
    right_real = right_jones[:, :, :, 0]
    right_imag = right_jones[:, :, :, 1]
    mixed_real = jnp.sum(
        left_real[:, :, :, None] * sky_real[:, None] - left_imag[:, :, :, None] * sky_imag[:, None],
        axis=2,
    )
    mixed_imag = jnp.sum(
        left_real[:, :, :, None] * sky_imag[:, None] + left_imag[:, :, :, None] * sky_real[:, None],
        axis=2,
    )
    out_real = jnp.sum(
        mixed_real[:, :, None] * right_real[:, None] + mixed_imag[:, :, None] * right_imag[:, None],
        axis=3,
    )
    out_imag = jnp.sum(
        mixed_imag[:, :, None] * right_real[:, None] - mixed_real[:, :, None] * right_imag[:, None],
        axis=3,
    )
    return (out_real.reshape(number, 4, SUB, SUB), out_imag.reshape(number, 4, SUB, SUB))


def transform(input_real, input_imag):
    series = jnp.arange(SUB, dtype=jnp.int32)
    turns = (series[:, None] * series[None, :] % SUB).astype(jnp.float32)
    table_real = jnp.cos(full_circle * turns / SUB)
    table_imag = -jnp.sin(full_circle * turns / SUB)
    best = lax.Precision.HIGHEST
    left_block = jnp.concatenate(
        [
            jnp.concatenate([table_real, -table_imag], axis=1),
            jnp.concatenate([table_imag, table_real], axis=1),
        ],
        axis=0,
    )
    right_block = jnp.concatenate(
        [
            jnp.concatenate([table_real, table_imag], axis=1),
            jnp.concatenate([-table_imag, table_real], axis=1),
        ],
        axis=0,
    )
    stacked = jnp.concatenate([input_real, input_imag], axis=2)
    inner = jnp.einsum("ka,npab->npkb", left_block, stacked, precision=best)
    joined = jnp.concatenate([inner[:, :, :SUB], inner[:, :, SUB:]], axis=3)
    outer = jnp.einsum("npkc,cq->npkq", joined, right_block, precision=best)
    return (outer[..., :SUB], outer[..., SUB:])


def subgrids_of(visibilities, item_records, screens, positions, channel_freq):
    number = visibilities.shape[0]
    east_phase_table, weighted_samples, station_one, station_two, interval = phase_tables(
        visibilities, item_records, positions, channel_freq, screens.shape[0]
    )
    jones_products = jnp.einsum(
        "qdg,qrg->qdr", east_phase_table, weighted_samples, preferred_element_type=jnp.float32
    )
    real_part, imag_part = correct(jones_products, screens, station_one, station_two, interval)
    outer_real, outer_imag = transform(real_part, imag_part)
    return jnp.stack([outer_real, outer_imag], axis=2).reshape(number, 8, SUB * SUB) / (SUB * SUB)


def place(grid_acc, subgrids, row_start, col_start):
    number = subgrids.shape[0]
    values = subgrids.reshape(number, 8, SUB, SUB)
    anchor = jnp.zeros((), jnp.int32)

    def add_window(index, acc):
        corner = (anchor, row_start[index], col_start[index])
        window = lax.dynamic_slice(acc, corner, (8, SUB, SUB))
        return lax.dynamic_update_slice(acc, window + values[index], corner)

    return lax.fori_loop(0, number, add_window, grid_acc)


def body(
    visibilities,
    screens,
    positions,
    channel_freq,
    owner_tile,
    baseline,
    time_block,
    row_in_tile,
    col_offset,
    valid_steps,
):
    peer_count = lax.axis_size("tile")
    local_items = visibilities.shape[0]
    capacity = max(2, 2 * local_items // peer_count)
    target = owner_tile[:, 0]
    onehot = (target[:, None] == jnp.arange(peer_count, dtype=jnp.int32)[None, :]).astype(jnp.int32)
    earlier = jnp.cumsum(onehot, axis=0) - onehot
    rank_in = jnp.sum(earlier * onehot, axis=1)
    slot_index = target * capacity + rank_in
    item_records = jnp.stack([baseline, time_block, row_in_tile, col_offset, valid_steps], axis=1)
    send_meta = jnp.zeros((peer_count * capacity, 5), jnp.int32).at[slot_index].set(item_records)
    send_meta = send_meta.reshape(peer_count, capacity, 5)
    send_vis = (
        jnp.zeros((peer_count * capacity, 8, NT * CH), jnp.bfloat16)
        .at[slot_index]
        .set(visibilities)
    )
    send_vis = send_vis.reshape(peer_count, capacity, 8, NT * CH)
    vis_in = lax.all_to_all(send_vis, "tile", split_axis=0, concat_axis=0, tiled=True)
    meta_in = lax.all_to_all(send_meta, "tile", split_axis=0, concat_axis=0, tiled=True)
    leading = vis_in.shape[:2]
    flat_grid = subgrids_of(
        vis_in.reshape((-1,) + vis_in.shape[2:]),
        meta_in.reshape(-1, 5),
        screens,
        positions,
        channel_freq,
    )
    landed_blocks = flat_grid.reshape(leading + flat_grid.shape[1:])
    flat_sub = landed_blocks.reshape(-1, 8, SUB * SUB)
    flat_meta = meta_in.reshape(-1, 5)
    buffer = place(
        jnp.zeros((8, STRIP + SUB, GCOLS), jnp.float32), flat_sub, flat_meta[:, 2], flat_meta[:, 3]
    )
    half_sub = SUB // 2
    extended = padded(buffer, (("tile", 1),), SUB // 2)
    result = extended[:, SUB : SUB + STRIP]
    result = result.at[:, :half_sub].add(extended[:, :half_sub])
    result = result.at[:, STRIP - half_sub :].add(extended[:, extended.shape[1] - half_sub :])
    return result


def solution(mesh):
    return jax.shard_map(
        body,
        mesh=mesh,
        in_specs=(
            P(("band", "tile"), None, None),
            P("band", None, None, None),
            P(),
            P("band"),
            P(("band", "tile"), None),
            P(("band", "tile")),
            P(("band", "tile")),
            P(("band", "tile")),
            P(("band", "tile")),
            P(("band", "tile")),
        ),
        out_specs=P("band", "tile", None),
        check_vma=False,
    )
```

profile of v0, /device:TPU:13, one launch (start us, length us, event | category | flops | bytes accessed | tf_op | source)
XLA Modules:
  0.0 744.8 jit_solution(3748852926444594644)
XLA Ops:
  4.3 6.6 all-to-all-start
  13.3 3.7 scatter_fusion
  17.1 6.0 all-to-all-start.1
  26.6 3.4 gather_fusion
  36.9 3.4 gather_fusion.3
  47.6 7.4 fusion.11
  57.4 3.6 fusion.13
  61.0 7.0 copy.83
  67.9 6.1 fusion.10
  90.6 14.7 %fusion.6 = f32[64,4,64,32]{0,2,3,1:T(8,128)S(1)} fusion(f32[64,4,32,32]{2,0,3,1:T(8,128)} %copy.94, f32[64,4,32,32]{2,0,3,1:T(8,128)} %copy.93, f32[32,32]{1,0:T(8,128)S(1)} %get-tuple-element.199, f32[32,32]{1,0:T(8,128)S(1)} %fusion.53, f32[32,32]{1,0:T(8,128)S(1)} %get-tuple-element.198), kind=kOutput, calls=%fused_computation.18 | convolution fusion | flops 403189760 | bytes 4206592 | tf_op jit(solution)/shard_map/ka,npab->npkb/dot_general | solution.py:177
  106.3 6.4 fusion.4
  116.9 9.1 %copy.98 = f32[64,8,32,32]{3,2,1,0:T(8,128)} copy(f32[64,8,32,32]{0,3,2,1:T(8,128)} %bitcast.77) | data formatting | bytes 4194304 | tf_op jit(solution)/shard_map/while | solution.py:206
  126.2 529.4 %while.15 = (s32[]{:T(128)}, f32[8,64,1024]{2,1,0:T(8,128)S(1)}, s32[64]{0:T(128)S(1)}, s32[64]{0:T(128)S(1)}, f32[64,8,32,32]{3,2,1,0:T(8,128)}, /*index=5*/s32[]{:T(128)}, s32[]{:T(128)}, s32[]{:T(128)}, s32[]{:T(128)}) while((s32[]{:T(128)}, f32[8,64,1024]{2,1,0:T(8,128)S(1)}, s32[64]{0:T(128)S(1)}, s32[64]{0:T(128)S(1)}, ...), condition=%wide.region_10.11_spmd, body=%wide.region_9.10_spmd.sunk | while | flops 8200 | bytes 164041 | solution.py:206
  132.4 3.3 dynamic_update_slice.8
  141.8 3.3 dynamic_update_slice.8
  165.5 3.3 dynamic_update_slice.8
  174.9 3.3 dynamic_update_slice.8
  198.6 3.1 dynamic_update_slice.8
  207.9 3.3 dynamic_update_slice.8
  238.6 3.3 dynamic_update_slice.8
  262.3 3.1 dynamic_update_slice.8
  271.6 3.3 dynamic_update_slice.8
  295.2 3.3 dynamic_update_slice.8
  304.7 3.4 dynamic_update_slice.8
  328.4 3.3 dynamic_update_slice.8
  337.8 3.3 dynamic_update_slice.8
  361.5 3.3 dynamic_update_slice.8
  371.0 3.3 dynamic_update_slice.8
  394.6 3.3 dynamic_update_slice.8
  404.1 3.3 dynamic_update_slice.8
  427.8 3.3 dynamic_update_slice.8
  437.3 3.3 dynamic_update_slice.8
  460.9 3.3 dynamic_update_slice.8
  470.4 3.3 dynamic_update_slice.8
  494.0 3.3 dynamic_update_slice.8
  503.4 3.3 dynamic_update_slice.8
  527.1 3.3 dynamic_update_slice.8
  536.6 3.3 dynamic_update_slice.8
  560.2 3.1 dynamic_update_slice.8
  569.5 3.3 dynamic_update_slice.8
  578.9 3.4 dynamic_update_slice.8
  595.5 3.3 dynamic_update_slice.8
  604.9 3.3 dynamic_update_slice.8
  628.6 3.3 dynamic_update_slice.8
  638.0 3.4 dynamic_update_slice.8
  655.7 75.4 %collective-permute-start = (f32[8,16,1024]{2,1,0:T(8,128)S(1)}, f32[8,16,1024]{2,1,0:T(8,128)S(1)}, u32[]{:S(2)}, u32[]{:S(2)}) collective-permute-start(f32[8,16,1024]{2,1,0:T(8,128)S(1)} %get-tuple-element.175), channel_id=1, source_target_pairs={{0,1},{1,2},{2,3},{3,4},{4,5},{5,6},{6,7},{7,8},{8,9},{9,10},{10,1... | collective-permute-start | bytes 1572872 | tf_op jit(solution)/shard_map/ppermute | solution.py:29
  733.1 4.1 collective-permute-done
  737.3 5.2 collective-permute-done.1
  (306 shorter events, 225.6 us)
Async XLA Ops:
  4.3 12.7 %all-to-all-start = ((s32[16,4,5]{2,1,0:T(4,128)}), s32[16,4,5]{2,1,0:T(4,128)S(1)}, u32[]{:S(2)}, u32[]{:S(2)}) async-start(s32[16,4,5]{2,1,0:T(4,128)} %bitcast.11), calls=%async_computation | async-start | bytes 65536 | tf_op jit(solution)/shard_map/all_to_all | solution.py:239
  17.1 37.9 %all-to-all-start.1 = ((bf16[16,4,8,128]{3,2,1,0:T(8,128)(2,1)}), bf16[16,4,8,128]{3,2,1,0:T(8,128)(2,1)S(1)}, u32[]{:S(2)}, u32[]{:S(2)}) async-start(bf16[16,4,8,128]{3,2,1,0:T(8,128)(2,1)} %bitcast.17), calls=%async_computation.1 | async-start | bytes 262144 | tf_op jit(solution)/shard_map/all_to_all | solution.py:238
  78.2 2.9 copy-start
  78.2 2.9 copy-start.1
  655.7 81.5 %collective-permute-start = (f32[8,16,1024]{2,1,0:T(8,128)S(1)}, f32[8,16,1024]{2,1,0:T(8,128)S(1)}, u32[]{:S(2)}, u32[]{:S(2)}) collective-permute-start(f32[8,16,1024]{2,1,0:T(8,128)S(1)} %get-tuple-element.175), channel_id=1, source_target_pairs={{0,1},{1,2},{2,3},{3,4},{4,5},{5,6},{6,7},{7,8},{8,9},{9,10},{10,1... | collective-permute-start | bytes 1572872 | tf_op jit(solution)/shard_map/ppermute | solution.py:29
  731.1 11.4 %collective-permute-start.1 = (f32[8,16,1024]{2,1,0:T(8,128)S(1)}, f32[8,16,1024]{2,1,0:T(8,128)S(1)}, u32[]{:S(2)}, u32[]{:S(2)}) collective-permute-start(f32[8,16,1024]{2,1,0:T(8,128)S(1)} %get-tuple-element.174), channel_id=1, source_target_pairs={{1,0},{2,1},{3,2},{4,3},{5,4},{6,5},{7,6},{8,7},{9,8},{10,9},{11,1... | collective-permute-start | bytes 1572872 | tf_op jit(solution)/shard_map/ppermute | solution.py:31
  737.3 5.2 copy-start.2
where the time goes:
time: 755 us; the launch traced here: 745 us
  local copies, waits for them, and re-layouts  277 us (37%)
  loops' own time  251 us (33%)
  other arithmetic  92.1 us (12%)
  starting transfers between devices  89.8 us (12%)
  matrix products  24.7 us (3%)
  waiting for transfers between devices  9.32 us (1%)
    another operation x1, loops' own time, place(): return lax.fori_loop(0, number, add_window, grid_acc)  251 us
    dynamic_update_slice x64, local copies, waits for them, and re-layouts, add_window(): return lax.dynamic_update_slice(acc, window + values[index], corner)  138 us
    dynamic_slice x128, local copies, waits for them, and re-layouts, add_window(): corner = (anchor, row_start[index], col_start[index])  75.4 us
    ppermute x1, starting transfers between devices, padded(): lax.ppermute(tail, axis, [(i, (i + 1) % count) for i in range(ends)])  75.4 us
    add x64, other arithmetic, add_window(): return lax.dynamic_update_slice(acc, window + values[index], corner)  65.1 us
  transfers between devices with their start and end apart: 4, of which 2 were waited for; matrix products, arithmetic and copies ran while one was open for 5% of the time, Pallas kernels for 0%

commit v1 on v0

v1 whole, which is shorter than its diff:
```python
import functools
import math

import jax
import jax.numpy as jnp
import numpy as np
from jax import lax
from jax.experimental import pallas as pl
from jax.experimental.pallas import tpu as pltpu
from jax.sharding import PartitionSpec as P

SUB = 32
NT = 2
BPER = 8
STRIP = 32
HALF = 16
LANES = 128
KINDS = 48

hour_step = 0.003
declination = -0.5

F32 = jnp.float32
BF16 = jnp.bfloat16
VMEM = pl.BlockSpec(memory_space=pltpu.VMEM)
SMEM = pl.BlockSpec(memory_space=pltpu.SMEM)
ANY = pl.BlockSpec(memory_space=pl.ANY)


def dft_tables():
    k8 = np.arange(8)
    turn = 2.0 * np.pi * np.outer(k8, k8) / 8.0
    c, s = np.cos(turn), np.sin(turn)
    eye = np.eye(4)
    inner = np.block([[np.kron(eye, c), np.kron(eye, s)], [-np.kron(eye, s), np.kron(eye, c)]])
    inner = np.concatenate([inner, inner], axis=1)
    m = np.arange(LANES) // SUB
    turn = 2.0 * np.pi * np.outer(k8, m) / 32.0
    twiddle = np.stack([np.cos(turn), -np.sin(turn)])
    b = np.arange(LANES) % SUB
    turn = 2.0 * np.pi * (np.outer(m, m) / 4.0 + np.outer(b, b) / 32.0)
    c, s = np.cos(turn) / 1024.0, np.sin(turn) / 1024.0
    outer = np.block([[c, -s], [s, c]]).astype(np.float32)
    high = outer.astype(jnp.bfloat16)
    low = (outer - high.astype(np.float32)).astype(jnp.bfloat16)
    return (
        jnp.asarray(inner.astype(jnp.bfloat16)),
        jnp.asarray(twiddle.astype(np.float32)),
        jnp.asarray(np.stack([high, low])),
    )


def pack_kernel(cap, owner, base, tick, row, col, steps, vis, out, scr, count):
    peers, rows, _ = out.shape
    items = vis.shape[0]
    scr[...] = jnp.zeros_like(scr)
    for t in range(peers):
        count[t] = 0
    lane = lax.broadcasted_iota(jnp.int32, (1, LANES), 1)
    for i in range(items):
        o = owner[i]
        r = count[o]
        count[o] = r + 1
        at = pl.multiple_of(o * rows + r * 8, 8)
        scr[pl.ds(at, 8), :] = vis[i].astype(F32)
        b = base[i]
        c = col[i]
        values = (b // 256, b % 256, tick[i], row[i], c // 8, c % 8, steps[i])
        meta = jnp.zeros((1, LANES), jnp.int32)
        for f, value in enumerate(values):
            meta = jnp.where(lane == f, value, meta)
        scr[pl.ds(o * rows + cap * 8 + r, 1), :] = meta.astype(F32)
    for t in range(peers):
        out[t] = scr[t * rows : (t + 1) * rows, :].astype(BF16)


def cos_sin_turns(x):
    x = x - jnp.round(x)
    quarter = jnp.round(x * 4.0)
    y = (x - quarter * 0.25) * (2.0 * math.pi)
    z = y * y
    s = y * (1.0 + z * (-1.0 / 6 + z * (1.0 / 120 + z * (-1.0 / 5040 + z * (1.0 / 362880)))))
    c = 1.0 + z * (-0.5 + z * (1.0 / 24 + z * (-1.0 / 720 + z * (1.0 / 40320 + z * (-1.0 / 3628800)))))
    odd = jnp.abs(quarter) == 1.0
    negative_c = (quarter == 1.0) | (jnp.abs(quarter) == 2.0)
    negative_s = (quarter == -1.0) | (jnp.abs(quarter) == 2.0)
    cos = jnp.where(odd, s, c)
    sin = jnp.where(odd, c, s)
    return jnp.where(negative_c, -cos, cos), jnp.where(negative_s, -sin, sin)


def cmul(a, b):
    return a[0] * b[0] - a[1] * b[1], a[0] * b[1] + a[1] * b[0]


def conj(a):
    return a[0], -a[1]


def both(a, b):
    rr, ii, ri, ir = a[0] * b[0], a[1] * b[1], a[0] * b[1], a[1] * b[0]
    return (rr - ii, ri + ir), (rr + ii, ir - ri)


def split(x):
    high = x.astype(BF16)
    return high, (x - high.astype(F32)).astype(BF16)


def main_kernel(
    cap, recv, positions, freq, inner, twiddle, outer, screens,
    strip, up, down,
    meta, index, table, sky, screen, plane, acc, place, screen_sem, index_sem,
):
    peers, rows, _ = recv.shape
    slots = peers * cap
    groups = slots // 8
    stations = positions.shape[0]
    intervals = screens.shape[0] // stations
    tiles = strip.shape[2] // LANES
    lane = lax.broadcasted_iota(jnp.int32, (8, LANES), 1)
    step = (lane // (LANES // NT)).astype(F32)

    for t in range(peers):
        chunk = recv[t, cap * 8 : cap * 8 + 8, :].astype(F32)
        meta[t * cap : (t + 1) * cap, :] = chunk[:cap, :]

    m = meta[...]
    baseline = m[:, 0:1] * 256.0 + m[:, 1:2]
    tick = m[:, 2:3]
    series = lax.broadcasted_iota(jnp.int32, (1, stations), 1).astype(F32)
    offsets = series * (2.0 * stations - series - 1.0) * 0.5
    one = jnp.sum((offsets <= baseline).astype(F32), axis=1, keepdims=True) - 1.0
    two = baseline - one * (2.0 * stations - one - 1.0) * 0.5 + one + 1.0
    interval = jnp.floor(tick * (1.0 / BPER))
    column = m[:, 4:5] * 8.0 + m[:, 5:6]
    tile_a = jnp.floor(column * (1.0 / LANES))
    lane_a = column - tile_a * LANES
    tile_b = jnp.floor((column - LANES // 2) * (1.0 / LANES))
    lane_b = column - LANES // 2 - tile_b * LANES
    fits = lane_a <= LANES - SUB
    values = (
        one * intervals + interval,
        two * intervals + interval,
        m[:, 3:4],
        jnp.where(fits, tile_a, tile_b + tiles),
        jnp.where(fits, lane_a, lane_b),
    )
    wide = lax.broadcasted_iota(jnp.int32, (slots, LANES), 1)
    packed = jnp.zeros((slots, LANES), F32)
    for f, value in enumerate(values):
        packed = jnp.where(wide == f, value, packed)
    index[...] = packed.astype(jnp.int32)
    to_scalar = pltpu.make_async_copy(index, place, index_sem)
    to_scalar.start()

    station = lax.broadcasted_iota(jnp.int32, (1, stations), 1).astype(F32)
    chosen = (station == two).astype(F32) - (station == one).astype(F32)
    vector = jnp.dot(chosen, positions[...], precision=lax.Precision.HIGHEST, preferred_element_type=F32)
    meta[:, 8:11] = vector

    to_scalar.wait()

    def fetch(n, _):
        for side in range(2):
            entry = place[n, side]
            pltpu.make_async_copy(screens.at[entry], screen.at[n, side], screen_sem).start()
        return 0

    lax.fori_loop(0, slots, fetch, 0)

    channel = jnp.concatenate([freq[...], freq[...]], axis=1)

    def phases(g, _):
        here = meta[pl.ds(pl.multiple_of(g * 8, 8), 8), :]
        start = here[:, 2:3] * NT
        live = (step < here[:, 6:7]).astype(F32)
        x, y, z = here[:, 8:9], here[:, 9:10], here[:, 10:11]
        scale = hour_step / (2.0 * math.pi)
        cos_now, sin_now = cos_sin_turns(scale * (start + step))
        cos_mid, sin_mid = cos_sin_turns(scale * (start + 0.5 * (NT - 1) + 0.0 * step))

        def track(c, s):
            u = s * x + c * y
            v = (-math.sin(declination)) * c * x + math.sin(declination) * s * y + math.cos(declination) * z
            return u, v

        u_now, v_now = track(cos_now, sin_now)
        u_mid, v_mid = track(cos_mid, sin_mid)
        du = (u_now * channel - u_mid) * (1.0 / SUB)
        dv = (v_now * channel - v_mid) * (1.0 / SUB)
        e1 = cos_sin_turns(0.5 * du)
        e2 = cmul(e1, e1)
        e3 = cmul(e2, e1)
        e4 = cmul(e2, e2)
        e8 = cmul(e4, e4)
        g1 = cos_sin_turns(dv)
        g2 = cmul(g1, g1)
        g3 = cmul(g2, g1)
        g4 = cmul(g2, g2)
        g8 = cmul(g4, g4)
        g12 = cmul(g8, g4)
        mid = (e3[0] * live, e3[1] * live)
        ups = [mid]
        for _ in range(3):
            ups.append(cmul(ups[-1], e8))
        downs = [cmul(mid, conj(e8))]
        for _ in range(3):
            downs.append(cmul(downs[-1], conj(e8)))
        row_phase = downs[::-1] + ups
        ones = (jnp.ones_like(du), jnp.zeros_like(du))
        col_phase = [conj(g4), conj(g3), conj(g2), conj(g1), ones, g1, g2, g3]
        base = pl.multiple_of(g * (KINDS * 8), 8)

        def put(kind, value):
            table[pl.ds(base + kind * 8, 8), :] = value

        for k in range(8):
            put(k, row_phase[k][0])
            put(8 + k, row_phase[k][1])
            put(16 + k, col_phase[k][0])
            put(24 + k, col_phase[k][1])
        k = 32
        for e in (e1, e3):
            plus12, minus12 = both(e, g12)
            plus4, minus4 = both(e, g4)
            for value in (minus12, minus4, plus4, plus12):
                put(k, value[0])
                put(k + 8, value[1])
                k += 1
        return 0

    lax.fori_loop(0, groups, phases, 0)

    def image(n, _):
        g = n // 8
        base = g * (KINDS * 8) + n % 8

        def rows_of(kind):
            return table[pl.ds(base + kind * 8, 8, stride=8), :]

        def row_of(kind):
            return table[pl.ds(base + kind * 8, 1), :]

        row_phase = (rows_of(0), rows_of(8))
        col_phase = (rows_of(16), rows_of(24))
        cells = [[None] * 4 for _ in range(4)]
        for k in range(8):
            mi, bb = k // 4, k % 4
            plus, minus = both(col_phase, (row_of(32 + k), row_of(40 + k)))
            cells[2 + mi][bb] = plus
            cells[1 - mi][3 - bb] = minus
        real = jnp.concatenate([cells[a][b][0] for a in range(4) for b in range(4)], axis=0)
        imag = jnp.concatenate([cells[a][b][1] for a in range(4) for b in range(4)], axis=0)
        right = jnp.concatenate([real.astype(BF16), imag.astype(BF16)], axis=1)
        peer = n // cap
        block = recv[peer, pl.ds(pl.multiple_of((n % cap) * 8, 8), 8), :].astype(F32)
        reals, imags = [], []
        for p in range(4):
            value = cmul(row_phase, (block[2 * p : 2 * p + 1, :], block[2 * p + 1 : 2 * p + 2, :]))
            reals.append(value[0])
            imags.append(value[1])
        real = jnp.concatenate(reals, axis=0)
        imag = jnp.concatenate(imags, axis=0)
        left = jnp.concatenate(
            [jnp.concatenate([real, -imag], axis=1), jnp.concatenate([imag, real], axis=1)], axis=0
        )
        high, low = split(left)
        dims = (((1,), (1,)), ((), ()))
        out = lax.dot_general(jnp.concatenate([high, low], axis=0), right, dims, preferred_element_type=F32)
        sky[n] = out[:64] + out[64:]
        return 0

    lax.fori_loop(0, slots, image, 0, unroll=2)

    acc[...] = jnp.zeros_like(acc)

    def land(n, _):
        for side in range(2):
            pltpu.make_async_copy(screens.at[0], screen.at[n, side], screen_sem).wait()
        return 0

    lax.fori_loop(0, slots, land, 0)

    batch = plane.shape[0]

    def grid(g, _):
        results = []
        for u in range(batch):
            n = g * batch + u
            jones = []
            for side in range(2):
                data = screen[n, side].astype(F32)
                for j in range(8):
                    plane[u, side, j * 8 : (j + 1) * 8, :] = data[:, j * LANES : (j + 1) * LANES]
                entry = [plane[u, side, pl.ds(e, 8, stride=8), :] for e in range(8)]
                jones.append([(entry[2 * k], entry[2 * k + 1]) for k in range(4)])
            image = sky[n]
            value = [(image[8 * p : 8 * p + 8], image[32 + 8 * p : 40 + 8 * p]) for p in range(4)]
            left, right = jones

            def add(a, b):
                return a[0] + b[0], a[1] + b[1]

            mixed = [
                add(cmul(left[2 * i], value[k]), cmul(left[2 * i + 1], value[2 + k]))
                for i in range(2)
                for k in range(2)
            ]
            corrected = [
                add(cmul(mixed[2 * i], conj(right[2 * j])), cmul(mixed[2 * i + 1], conj(right[2 * j + 1])))
                for i in range(2)
                for j in range(2)
            ]
            stacked = jnp.concatenate([c[0] for c in corrected] + [c[1] for c in corrected], axis=0)
            high, low = split(stacked)
            turned = jnp.dot(inner[...], jnp.concatenate([high, low], axis=0), preferred_element_type=F32)
            tw = (twiddle[0], twiddle[1])
            spun = [cmul((turned[8 * p : 8 * p + 8], turned[32 + 8 * p : 40 + 8 * p]), tw) for p in range(4)]
            results.append(
                jnp.concatenate(
                    [jnp.concatenate([s[0] for s in spun], axis=0), jnp.concatenate([s[1] for s in spun], axis=0)],
                    axis=1,
                )
            )
        high, low = split(jnp.concatenate(results, axis=0))
        out = jnp.dot(high, outer[0], preferred_element_type=F32)
        out += jnp.dot(high, outer[1], preferred_element_type=F32)
        out += jnp.dot(low, outer[0], preferred_element_type=F32)
        for u in range(batch):
            n = g * batch + u
            first = place[n, 2]
            tile = place[n, 3]
            shift = place[n, 4]
            inside = (lane >= shift) & (lane < shift + SUB)
            for p in range(4):
                for r in range(2):
                    cell = out[u * 32 + 8 * p : u * 32 + 8 * p + 8, r * LANES : (r + 1) * LANES]
                    parts = []
                    for k4 in range(4):
                        turn = (shift + (LANES - SUB * k4)) % LANES
                        parts.append(jnp.where(inside, pltpu.roll(cell, turn, 1), 0.0))
                    spot = (tile, 2 * p + r, pl.ds(first, SUB), slice(None))
                    acc[spot] = acc[spot] + jnp.concatenate(parts, axis=0)
        return 0

    lax.fori_loop(0, slots // batch, grid, 0)

    half = lax.broadcasted_iota(jnp.int32, (STRIP + SUB, LANES), 1) < LANES // 2
    for plane_at in range(8):
        behind = None
        for t in range(tiles):
            value = acc[t, plane_at]
            turned = None
            if t < tiles - 1:
                turned = pltpu.roll(acc[tiles + t, plane_at], LANES // 2, 1)
                value = value + jnp.where(half, 0.0, turned)
            if behind is not None:
                value = value + jnp.where(half, behind, 0.0)
            behind = turned
            columns = slice(t * LANES, (t + 1) * LANES)
            up[plane_at, :, columns] = value[:HALF].astype(BF16)
            strip[plane_at, :, columns] = value[HALF : HALF + STRIP]
            down[plane_at, :, columns] = value[HALF + STRIP :].astype(BF16)


def add_kernel(strip, above, below, out):
    out[:, :HALF, :] = strip[:, :HALF, :] + above[...].astype(F32)
    out[:, HALF:, :] = strip[:, HALF:, :] + below[...].astype(F32)


def body(visibilities, screens, positions, channel_freq, owner, baseline, tick, row, col, steps):
    peers = lax.axis_size("tile")
    items = visibilities.shape[0]
    cap = max(2, 2 * items // peers)
    slots = peers * cap
    rows = cap * 8 + 8
    columns = 1024
    tiles = columns // LANES

    packed = pl.pallas_call(
        functools.partial(pack_kernel, cap),
        out_shape=jax.ShapeDtypeStruct((peers, rows, LANES), BF16),
        in_specs=[SMEM] * 6 + [VMEM],
        out_specs=VMEM,
        scratch_shapes=[pltpu.VMEM((peers * rows, LANES), F32), pltpu.SMEM((peers,), jnp.int32)],
        name="pack",
    )(owner[:, 0], baseline, tick, row, col, steps, visibilities)
    received = lax.all_to_all(packed, "tile", split_axis=0, concat_axis=0, tiled=True)

    inner, twiddle, outer = dft_tables()
    table = screens.reshape(screens.shape[0] * screens.shape[1], 8, SUB * SUB)
    batch = 4
    strip, up, down = pl.pallas_call(
        functools.partial(main_kernel, cap),
        out_shape=(
            jax.ShapeDtypeStruct((8, STRIP, columns), F32),
            jax.ShapeDtypeStruct((8, HALF, columns), BF16),
            jax.ShapeDtypeStruct((8, HALF, columns), BF16),
        ),
        in_specs=[VMEM] * 6 + [ANY],
        out_specs=(VMEM, VMEM, VMEM),
        scratch_shapes=[
            pltpu.VMEM((slots, LANES), F32),
            pltpu.VMEM((slots, LANES), jnp.int32),
            pltpu.VMEM((slots * KINDS, LANES), F32),
            pltpu.VMEM((slots, 64, LANES), F32),
            pltpu.VMEM((slots, 2, 8, SUB * SUB), BF16),
            pltpu.VMEM((batch, 2, 64, LANES), F32),
            pltpu.VMEM((2 * tiles - 1, 8, STRIP + SUB, LANES), F32),
            pltpu.SMEM((slots, LANES), jnp.int32),
            pltpu.SemaphoreType.DMA,
            pltpu.SemaphoreType.DMA,
        ],
        compiler_params=pltpu.CompilerParams(vmem_limit_bytes=40 * 1024 * 1024),
        name="grid_items",
    )(received, positions, channel_freq[None, :], inner, twiddle, outer, table)

    ends = peers - 1
    above = lax.ppermute(down, "tile", [(i, i + 1) for i in range(ends)])
    below = lax.ppermute(up, "tile", [(i + 1, i) for i in range(ends)])
    return pl.pallas_call(
        add_kernel,
        out_shape=jax.ShapeDtypeStruct(strip.shape, F32),
        in_specs=[VMEM] * 3,
        out_specs=VMEM,
        name="add_spill",
    )(strip, above, below)


def solution(mesh):
    return jax.shard_map(
        body,
        mesh=mesh,
        in_specs=(
            P(("band", "tile"), None, None),
            P("band", None, None, None),
            P(),
            P("band"),
            P(("band", "tile"), None),
            P(("band", "tile")),
            P(("band", "tile")),
            P(("band", "tile")),
            P(("band", "tile")),
            P(("band", "tile")),
        ),
        out_specs=P("band", "tile", None),
        check_vma=False,
    )
```

time: 755 us -> 60.3 us (0.08); the launches traced: 745 us -> 59.8 us
  local copies, waits for them, and re-layouts: 277 us -> 8.32 us
  loops' own time: 251 us -> 0 us
  other arithmetic: 92.1 us -> 0 us
  starting transfers between devices: 89.8 us -> 12.1 us
  Pallas kernels: 0 us -> 27.6 us
  matrix products: 24.7 us -> 0 us
    another operation x1 -> x0, loops' own time: 251 us -> none  [place(): return lax.fori_loop(0, number, add_window, grid_acc)]
    dynamic_update_slice x64 -> x0, local copies, waits for them, and re-layouts: 138 us -> none  [add_window(): return lax.dynamic_update_slice(acc, window + values[index], corner)]
    dynamic_slice x128 -> x0, local copies, waits for them, and re-layouts: 75.4 us -> none  [add_window(): corner = (anchor, row_start[index], col_start[index])]
    ppermute x2, starting transfers between devices: 77.3 us -> 5.57 us  [the longest x1 3.65 us: body(): above = lax.ppermute(down, 'tile', [(i, i + 1) for i in range(ends)])]
    add x67 -> x0, other arithmetic: 65.6 us -> none  [the longest x64 65.1 us: add_window(): return lax.dynamic_update_slice(acc, window + values[index], corner)]
    pallas_call x0 -> x3, Pallas kernels: none -> 27.6 us  [the longest x1 23.2 us: body(): pl.pallas_call(functools.partial(main_kernel, cap), out_shape=(jax.ShapeD...]
    dot_general x3 -> x0, matrix products: 24.7 us -> none  [the longest x1 14.7 us: transform(): inner = jnp.einsum('ka,npab->npkb', left_block, stacked, precision=best)]
    another operation x4 -> x0, other arithmetic: 9.5 us -> none
  transfers between devices with their start and end apart: 4 -> 3, of which waited for: 2 -> 3; matrix products, arithmetic and copies ran while one was open for 5% -> 1% of each run, Pallas kernels for 0% -> 0%
where the time goes in v1:
time: 60.3 us; the launch traced here: 59.8 us
  Pallas kernels  27.6 us (46%)
  starting transfers between devices  12.1 us (20%)
  waiting for transfers between devices  11.7 us (19%)
  local copies, waits for them, and re-layouts  8.32 us (14%)
    pallas_call x1, Pallas kernels, body(): pl.pallas_call(functools.partial(main_kernel, cap), out_shape=(jax.ShapeD...  23.2 us
    unnamed x17, local copies, waits for them, and re-layouts  8.32 us
    all_to_all x1, starting transfers between devices, body(): lax.all_to_all(packed, 'tile', split_axis=0, concat_axis=0, tiled=True)  6.56 us
    ppermute x1, waiting for transfers between devices, body(): below = lax.ppermute(up, 'tile', [(i + 1, i) for i in range(ends)])  5.29 us
    all_to_all x1, waiting for transfers between devices, body(): lax.all_to_all(packed, 'tile', split_axis=0, concat_axis=0, tiled=True)  5.04 us
    ppermute x1, starting transfers between devices, body(): above = lax.ppermute(down, 'tile', [(i, i + 1) for i in range(ends)])  3.65 us
    pallas_call x1, Pallas kernels, body(): pl.pallas_call(add_kernel, out_shape=jax.ShapeDtypeStruct(strip.shape, F3...  2.4 us
    pallas_call x1, Pallas kernels, body(): pl.pallas_call(functools.partial(pack_kernel, cap), out_shape=jax.ShapeDt...  2 us
  transfers between devices with their start and end apart: 3, of which 3 were waited for; matrix products, arithmetic and copies ran while one was open for 1% of the time, Pallas kernels for 0%

profile of v1, /device:TPU:13, one launch (start us, length us, event | category | flops | bytes accessed | tf_op | source)
XLA Modules:
  0.0 59.8 jit_solution(9771055555088150025)
XLA Ops:
  0.0 2.0 %pack.1 = bf16[16,40,128]{2,1,0:T(8,128)(2,1)} custom-call(s32[32]{0:T(128)} %bitcast.5, s32[32]{0:T(128)} %base.1, s32[32]{0:T(128)} %tick.1, s32[32]{0:T(128)} %row.1, s32[32]{0:T(128)} %col.1, s32[32]{0:T(128)} %steps.1, bf16[32,8,128]{2,1,0:T(8,128)(2,1)} %vis.1), custom_call_target="tpu_custom_call" | custom-call | tf_op jit(solution)/shard_map/pack/pallas_call | solution.py:381
  2.0 6.6 %all-to-all-start = ((bf16[16,40,128]{2,1,0:T(8,128)(2,1)}), bf16[16,40,128]{2,1,0:T(8,128)(2,1)S(1)}, u32[]{:S(2)}, u32[]{:S(2)}) async-start(bf16[16,40,128]{2,1,0:T(8,128)(2,1)} %pack.1), calls=%async_computation | async-start | bytes 327680 | tf_op jit(solution)/shard_map/all_to_all | solution.py:389
  8.6 0.8 %copy.14.positions = f32[197,3]{1,0:T(8,128)S(1)} copy(f32[197,3]{0,1:T(4,128)} %param.15) | data formatting | bytes 4728 | tf_op args[2]
  9.4 5.0 %all-to-all-done.recv = bf16[16,40,128]{2,1,0:T(8,128)(2,1)S(1)} async-done(((bf16[16,40,128]{2,1,0:T(8,128)(2,1)}), bf16[16,40,128]{2,1,0:T(8,128)(2,1)S(1)}, u32[]{:S(2)}, u32[]{:S(2)}) %all-to-all-start) | async-done | bytes 163872 | tf_op jit(solution)/shard_map/all_to_all | solution.py:389
  14.4 0.0 copy-start
  14.4 2.8 %copy-done = bf16[197,2,8,1024]{3,2,1,0:T(8,128)(2,1)S(1)} copy-done((bf16[197,2,8,1024]{3,2,1,0:T(8,128)(2,1)S(1)}, bf16[197,2,8,1024]{3,2,1,0:T(8,128)(2,1)}, u32[]{:S(2)}) %copy-start) | copy-done | bytes 6455320
  17.2 0.0 copy-start.2
  17.2 0.9 %copy-done.2 = bf16[2,256,256]{2,1,0:T(8,128)(2,1)S(1)} copy-done((bf16[2,256,256]{2,1,0:T(8,128)(2,1)S(1)}, bf16[2,256,256]{2,1,0:T(8,128)(2,1)}, u32[]{:S(2)}) %copy-start.2) | copy-done | bytes 262168
  18.2 0.0 copy-start.3
  18.2 0.7 %copy-done.3 = bf16[64,128]{1,0:T(8,128)(2,1)S(1)} copy-done((bf16[64,128]{1,0:T(8,128)(2,1)S(1)}, bf16[64,128]{1,0:T(8,128)(2,1)}, u32[]{:S(2)}) %copy-start.3) | copy-done | bytes 16408
  18.9 0.0 copy-start.4
  18.9 0.7 %copy-done.4 = f32[2,8,128]{2,1,0:T(8,128)S(1)} copy-done((f32[2,8,128]{2,1,0:T(8,128)S(1)}, f32[2,8,128]{2,1,0:T(8,128)}, u32[]{:S(2)}) %copy-start.4) | copy-done | bytes 8216
  19.6 0.0 copy-start.5
  19.6 0.7 %copy-done.5 = f32[64]{0:T(128)S(1)} copy-done((f32[64]{0:T(128)S(1)}, f32[64]{0:T(128)}, u32[]{:S(2)}) %copy-start.5) | copy-done | bytes 280
  20.3 23.2 %grid_items.1 = (f32[8,32,1024]{2,1,0:T(8,128)S(1)}, bf16[8,16,1024]{2,1,0:T(8,128)(2,1)S(1)}, bf16[8,16,1024]{2,1,0:T(8,128)(2,1)S(1)}) custom-call(bf16[16,40,128]{2,1,0:T(8,128)(2,1)S(1)} %all-to-all-done.recv, f32[197,3]{1,0:T(8,128)S(1)} %copy.14.positions, f32[1,64]{1,0:T(1,128)S(1)} %bitcast.4, bf16[64,128]{1,0:T(8,128)(2,1)S(1)} %copy-done.3, ...), custom_call_target="tpu_custom_call" | custom-call | tf_op jit(solution)/shard_map/grid_items/pallas_call | solution.py:394
  43.5 0.0 copy-start.1
  43.5 1.0 %copy-done.1 = f32[8,32,1024]{2,1,0:T(8,128)} copy-done((f32[8,32,1024]{2,1,0:T(8,128)}, f32[8,32,1024]{2,1,0:T(8,128)S(1)}, u32[]{:S(2)}) %copy-start.1) | copy-done | bytes 1048600
  44.4 3.6 %collective-permute-start = (bf16[8,16,1024]{2,1,0:T(8,128)(2,1)S(1)}, bf16[8,16,1024]{2,1,0:T(8,128)(2,1)S(1)}, u32[]{:S(2)}, u32[]{:S(2)}) collective-permute-start(bf16[8,16,1024]{2,1,0:T(8,128)(2,1)S(1)} %get-tuple-element.9), channel_id=1, source_target_pairs={{0,1},{1,2},{2,3},{3,4},{4,5},{5,6},{6,7},{7,8},{8,9},{9,10},{10,1... | collective-permute-start | bytes 786440 | tf_op jit(solution)/shard_map/ppermute | solution.py:420
  48.1 1.9 %collective-permute-start.1 = (bf16[8,16,1024]{2,1,0:T(8,128)(2,1)S(1)}, bf16[8,16,1024]{2,1,0:T(8,128)(2,1)S(1)}, u32[]{:S(2)}, u32[]{:S(2)}) collective-permute-start(bf16[8,16,1024]{2,1,0:T(8,128)(2,1)S(1)} %get-tuple-element.10), channel_id=1, source_target_pairs={{1,0},{2,1},{3,2},{4,3},{5,4},{6,5},{7,6},{8,7},{9,8},{10,9},{11,1... | collective-permute-start | bytes 786440 | tf_op jit(solution)/shard_map/ppermute | solution.py:421
  50.0 1.4 %collective-permute-done.above = bf16[8,16,1024]{2,1,0:T(8,128)(2,1)S(1)} collective-permute-done((bf16[8,16,1024]{2,1,0:T(8,128)(2,1)S(1)}, bf16[8,16,1024]{2,1,0:T(8,128)(2,1)S(1)}, u32[]{:S(2)}, u32[]{:S(2)}) %collective-permute-start) | collective-permute-done | bytes 262176 | tf_op jit(solution)/shard_map/ppermute | solution.py:420
  51.4 0.0 copy-start.6
  51.4 5.3 %collective-permute-done.1.below = bf16[8,16,1024]{2,1,0:T(8,128)(2,1)S(1)} collective-permute-done((bf16[8,16,1024]{2,1,0:T(8,128)(2,1)S(1)}, bf16[8,16,1024]{2,1,0:T(8,128)(2,1)S(1)}, u32[]{:S(2)}, u32[]{:S(2)}) %collective-permute-start.1) | collective-permute-done | bytes 262176 | tf_op jit(solution)/shard_map/ppermute | solution.py:421
  56.7 0.0 copy-start.7
  56.7 0.0 copy-done.6
  56.7 0.7 %copy-done.7 = bf16[8,16,1024]{2,1,0:T(8,128)(2,1)} copy-done((bf16[8,16,1024]{2,1,0:T(8,128)(2,1)}, bf16[8,16,1024]{2,1,0:T(8,128)(2,1)S(1)}, u32[]{:S(2)}) %copy-start.7) | copy-done | bytes 262168
  57.4 2.4 %add_spill.1 = f32[8,32,1024]{2,1,0:T(8,128)} custom-call(f32[8,32,1024]{2,1,0:T(8,128)} %copy-done.1, bf16[8,16,1024]{2,1,0:T(8,128)(2,1)} %copy-done.6, bf16[8,16,1024]{2,1,0:T(8,128)(2,1)} %copy-done.7), custom_call_target="tpu_custom_call" | custom-call | tf_op jit(solution)/shard_map/add_spill/pallas_call | solution.py:422
Async XLA Ops:
  2.0 12.4 %all-to-all-start = ((bf16[16,40,128]{2,1,0:T(8,128)(2,1)}), bf16[16,40,128]{2,1,0:T(8,128)(2,1)S(1)}, u32[]{:S(2)}, u32[]{:S(2)}) async-start(bf16[16,40,128]{2,1,0:T(8,128)(2,1)} %pack.1), calls=%async_computation | async-start | bytes 327680 | tf_op jit(solution)/shard_map/all_to_all | solution.py:389
  14.4 2.8 %copy-start = (bf16[197,2,8,1024]{3,2,1,0:T(8,128)(2,1)S(1)}, bf16[197,2,8,1024]{3,2,1,0:T(8,128)(2,1)}, u32[]{:S(2)}) copy-start(bf16[197,2,8,1024]{3,2,1,0:T(8,128)(2,1)} %param.14) | copy-start | bytes 19365892
  17.2 0.9 %copy-start.2 = (bf16[2,256,256]{2,1,0:T(8,128)(2,1)S(1)}, bf16[2,256,256]{2,1,0:T(8,128)(2,1)}, u32[]{:S(2)}) copy-start(bf16[2,256,256]{2,1,0:T(8,128)(2,1)} %constant.8.clone.outer) | copy-start | bytes 786436
  18.2 0.7 %copy-start.3 = (bf16[64,128]{1,0:T(8,128)(2,1)S(1)}, bf16[64,128]{1,0:T(8,128)(2,1)}, u32[]{:S(2)}) copy-start(bf16[64,128]{1,0:T(8,128)(2,1)} %constant.6.clone.inner) | copy-start | bytes 49156
  18.9 0.7 %copy-start.4 = (f32[2,8,128]{2,1,0:T(8,128)S(1)}, f32[2,8,128]{2,1,0:T(8,128)}, u32[]{:S(2)}) copy-start(f32[2,8,128]{2,1,0:T(8,128)} %constant.7.clone.twiddle) | copy-start | bytes 24580
  19.6 0.7 %copy-start.5 = (f32[64]{0:T(128)S(1)}, f32[64]{0:T(128)}, u32[]{:S(2)}) copy-start(f32[64]{0:T(128)} %param.16) | copy-start | bytes 772
  43.5 1.0 %copy-start.1 = (f32[8,32,1024]{2,1,0:T(8,128)}, f32[8,32,1024]{2,1,0:T(8,128)S(1)}, u32[]{:S(2)}) copy-start(f32[8,32,1024]{2,1,0:T(8,128)S(1)} %get-tuple-element.8.strip) | copy-start | bytes 3145732
  44.4 6.9 %collective-permute-start = (bf16[8,16,1024]{2,1,0:T(8,128)(2,1)S(1)}, bf16[8,16,1024]{2,1,0:T(8,128)(2,1)S(1)}, u32[]{:S(2)}, u32[]{:S(2)}) collective-permute-start(bf16[8,16,1024]{2,1,0:T(8,128)(2,1)S(1)} %get-tuple-element.9), channel_id=1, source_target_pairs={{0,1},{1,2},{2,3},{3,4},{4,5},{5,6},{6,7},{7,8},{8,9},{9,10},{10,1... | collective-permute-start | bytes 786440 | tf_op jit(solution)/shard_map/ppermute | solution.py:420
  48.1 8.6 %collective-permute-start.1 = (bf16[8,16,1024]{2,1,0:T(8,128)(2,1)S(1)}, bf16[8,16,1024]{2,1,0:T(8,128)(2,1)S(1)}, u32[]{:S(2)}, u32[]{:S(2)}) collective-permute-start(bf16[8,16,1024]{2,1,0:T(8,128)(2,1)S(1)} %get-tuple-element.10), channel_id=1, source_target_pairs={{1,0},{2,1},{3,2},{4,3},{5,4},{6,5},{7,6},{8,7},{9,8},{10,9},{11,1... | collective-permute-start | bytes 786440 | tf_op jit(solution)/shard_map/ppermute | solution.py:421
  51.4 5.3 %copy-start.6 = (bf16[8,16,1024]{2,1,0:T(8,128)(2,1)}, bf16[8,16,1024]{2,1,0:T(8,128)(2,1)S(1)}, u32[]{:S(2)}) copy-start(bf16[8,16,1024]{2,1,0:T(8,128)(2,1)S(1)} %collective-permute-done.above) | copy-start | bytes 786436
  56.7 0.7 %copy-start.7 = (bf16[8,16,1024]{2,1,0:T(8,128)(2,1)}, bf16[8,16,1024]{2,1,0:T(8,128)(2,1)S(1)}, u32[]{:S(2)}) copy-start(bf16[8,16,1024]{2,1,0:T(8,128)(2,1)S(1)} %collective-permute-done.1.below) | copy-start | bytes 786436
